TPU v7x, 32 devices: a whole 2x2x4 slice. The times are simulated.
32 devices in a mesh: ep: 4 (over y, x), edp: 8 (over z, core).
Axes of the slice: x: 2, y: 2, z: 4, core: 2. Of those that a mesh axis runs over, the one named last changes fastest.
Arguments:
- tokens: bfloat16 [512, 4096], P('ep', 'edp'), may hold values from -6 to 6
- out_grad: bfloat16 [512, 4096], P('ep', 'edp'), may hold values from -1.5 to 1.5
- probs: float32 [512, 8], P('ep'), may hold values from 0.1 to 1
- expert_ids: int32 [512, 8], P('ep'), may hold values from 0 to 127, all different within a row; in each aligned block of 128 rows (0 to 127, 128 to 255, ...) at most 16 rows name the same one
- w_gate: bfloat16 [8, 4096, 1024], P('edp', 'ep'), may hold values from -0.09375 to 0.09375
- w_up: bfloat16 [8, 4096, 1024], P('edp', 'ep'), may hold values from -0.09375 to 0.09375
- w_down: bfloat16 [8, 1024, 4096], P('edp', None, 'ep'), may hold values from -0.1875 to 0.1875
Outputs:
- token_grad: bfloat16 [512, 4096], P('ep', 'edp')
- grad_gate: bfloat16 [8, 4096, 1024], P('edp', 'ep')
- grad_up: bfloat16 [8, 4096, 1024], P('edp', 'ep')
- grad_down: bfloat16 [8, 1024, 4096], P('edp', None, 'ep')
Inputs may be any that keep to these rules, and one draw needn't show every extreme that they name: `expert_ids`: each row names 8 different experts; within each context block of 128 tokens no expert is named by more than 16 tokens, a bound that some block reaches.
All inputs are finite; a program needn't handle non-finite values.
Results may differ from a plain program's by a relative error of at most 0.0058.
Values may be sent and summed in bfloat16 or wider, within the bound.
A program may use at most 64 MiB of HBM per device.

v0:
```python
import jax
import jax.numpy as jnp
from jax import lax
from jax.sharding import PartitionSpec as P

CAP = 16


def swiglu_back(gate_sum, up_sum, back_sum, weight_col):
    sigmoid_gate = jax.nn.sigmoid(gate_sum)
    silu_gate = gate_sum * sigmoid_gate
    hidden_grad = weight_col * back_sum
    hidden_weighted = (weight_col * silu_gate * up_sum).astype(jnp.bfloat16)
    up_grad = (hidden_grad * silu_gate).astype(jnp.bfloat16)
    gate_grad = (
        hidden_grad * up_sum * sigmoid_gate * (1.0 + gate_sum * (1.0 - sigmoid_gate))
    ).astype(jnp.bfloat16)
    return (gate_grad, up_grad, hidden_weighted)


def per_device(tokens, out_grad, probs, expert_ids, w_gate, w_up, w_down):
    tok_rows = tokens.shape[0]
    picks_each = expert_ids.shape[1]
    windows = lax.axis_size("edp")
    capacity = CAP
    slot_total = windows * capacity
    flat_ids = expert_ids.reshape(-1)
    flat_probs = probs.reshape(-1)
    onehot_ids = (flat_ids[:, None] == jnp.arange(windows, dtype=jnp.int32)[None, :]).astype(
        jnp.int32
    )
    ranking = jnp.sum((jnp.cumsum(onehot_ids, axis=0) - onehot_ids) * onehot_ids, axis=1)
    inside = jnp.sum(onehot_ids, axis=1)
    slot_code = jnp.where(inside > 0, flat_ids * capacity + ranking, -1)
    matches = slot_code[:, None] == jnp.arange(slot_total, dtype=jnp.int32)[None, :]
    per_token = jnp.any(matches.reshape(tok_rows, picks_each, slot_total), axis=1)
    dispatch_matrix = per_token.T.astype(jnp.bfloat16)
    slot_weights = jnp.sum(jnp.where(matches, flat_probs[:, None], 0.0), axis=0)
    my_expert = lax.axis_index("edp")
    share_weight = lax.dynamic_slice_in_dim(slot_weights, my_expert * capacity, capacity, 0)
    tok_block = jnp.dot(dispatch_matrix, tokens, preferred_element_type=jnp.float32).astype(
        jnp.bfloat16
    )
    grad_block = jnp.dot(dispatch_matrix, out_grad, preferred_element_type=jnp.float32).astype(
        jnp.bfloat16
    )
    tok_block = tok_block.reshape(windows, capacity, tokens.shape[1])
    grad_block = grad_block.reshape(windows, capacity, tokens.shape[1])
    slot_tokens, slot_grads = (
        lax.all_to_all(
            lax.all_to_all(tok_block, "edp", split_axis=0, concat_axis=2, tiled=True),
            "ep",
            split_axis=2,
            concat_axis=1,
            tiled=True,
        ),
        lax.all_to_all(
            lax.all_to_all(grad_block, "edp", split_axis=0, concat_axis=2, tiled=True),
            "ep",
            split_axis=2,
            concat_axis=1,
            tiled=True,
        ),
    )
    slot_tokens = slot_tokens[0]
    slot_grads = slot_grads[0]
    gate_local = w_gate[0]
    up_local = w_up[0]
    down_local = w_down[0]
    hidden_units = gate_local.shape[1]
    contract_last = (((1,), (1,)), ((), ()))
    summed = lax.psum_scatter(
        jnp.concatenate(
            [
                jnp.dot(slot_tokens, gate_local, preferred_element_type=jnp.float32),
                jnp.dot(slot_tokens, up_local, preferred_element_type=jnp.float32),
                lax.dot_general(
                    slot_grads, down_local, contract_last, preferred_element_type=jnp.float32
                ),
            ],
            axis=1,
        ),
        "ep",
        scatter_dimension=0,
        tiled=True,
    )
    gate_sum = summed[:, :hidden_units]
    up_sum = summed[:, hidden_units : 2 * hidden_units]
    back_sum = summed[:, 2 * hidden_units :]
    gate_grad, up_grad, hidden_weighted = swiglu_back(
        gate_sum, up_sum, back_sum, share_weight[:, None]
    )
    gate_grad, up_grad, hidden_weighted = (
        lax.all_gather(gate_grad, "ep", axis=0, tiled=True),
        lax.all_gather(up_grad, "ep", axis=0, tiled=True),
        lax.all_gather(hidden_weighted, "ep", axis=0, tiled=True),
    )
    slot_grad = (
        lax.dot_general(gate_grad, gate_local, contract_last, preferred_element_type=jnp.float32)
        + lax.dot_general(up_grad, up_local, contract_last, preferred_element_type=jnp.float32)
    ).astype(jnp.bfloat16)
    contract_first = (((0,), (0,)), ((), ()))
    grad_gate = lax.dot_general(
        slot_tokens, gate_grad, contract_first, preferred_element_type=jnp.float32
    ).astype(jnp.bfloat16)
    grad_up = lax.dot_general(
        slot_tokens, up_grad, contract_first, preferred_element_type=jnp.float32
    ).astype(jnp.bfloat16)
    grad_down = lax.dot_general(
        hidden_weighted, slot_grads, contract_first, preferred_element_type=jnp.float32
    ).astype(jnp.bfloat16)
    returned = lax.all_to_all(
        lax.all_to_all(slot_grad[None], "ep", split_axis=1, concat_axis=2, tiled=True),
        "edp",
        split_axis=2,
        concat_axis=0,
        tiled=True,
    )
    returned = returned.reshape(slot_total, tokens.shape[1])
    token_grad = lax.dot_general(
        dispatch_matrix, returned, contract_first, preferred_element_type=jnp.float32
    ).astype(jnp.bfloat16)
    return (token_grad, grad_gate[None], grad_up[None], grad_down[None])


def solution(mesh):
    placed = (
        P("ep", "edp"),
        P("ep", "edp"),
        P("ep", None),
        P("ep", None),
        P("edp", "ep", None),
        P("edp", "ep", None),
        P("edp", None, "ep"),
    )
    return jax.shard_map(
        per_device,
        mesh=mesh,
        in_specs=placed,
        out_specs=(
            P("ep", "edp"),
            P("edp", "ep", None),
            P("edp", "ep", None),
            P("edp", None, "ep"),
        ),
        check_vma=False,
    )
```

profile of v0, /device:TPU:0, one launch (start us, length us, event | category | flops | bytes accessed | tf_op | source)
XLA Modules:
  0.0 241.3 jit_solution(4901406480410002356)
XLA Ops:
  7.2 0.9 copy.71
  8.1 0.1 eq.45
  8.2 0.1 eq.49
  8.3 2.3 reduce-window.6
  10.6 0.3 slice_reduce_fusion
  10.9 0.2 reduce-window.9
  11.0 0.1 add_bitcast_fusion
  11.1 0.1 reduce_sum.31
  11.2 0.6 add_select_fusion
  11.8 0.1 gt.16
  12.1 0.7 add_select_fusion.1
  12.8 0.1 copy.75
  12.9 0.3 fusion.19
  13.1 1.8 convolution_convert_fusion.2
  14.9 6.3 %all-to-all-start = ((bf16[8,16,512]{2,1,0:T(8,128)(2,1)}), bf16[8,16,512]{2,1,0:T(8,128)(2,1)S(1)}, u32[]{:S(2)}, u32[]{:S(2)}) async-start(bf16[8,16,512]{2,1,0:T(8,128)(2,1)} %bitcast.1), calls=%async_computation | async-start | bytes 262144 | tf_op jit(solution)/shard_map/all_to_all | solution.py:51
  21.3 1.8 convolution_convert_fusion.1
  23.1 5.0 %all-to-all-done = bf16[8,16,512]{2,1,0:T(8,128)(2,1)S(1)} async-done(((bf16[8,16,512]{2,1,0:T(8,128)(2,1)}), bf16[8,16,512]{2,1,0:T(8,128)(2,1)S(1)}, u32[]{:S(2)}, u32[]{:S(2)}) %all-to-all-start) | async-done | bytes 131104 | tf_op jit(solution)/shard_map/all_to_all | solution.py:51
  28.0 3.4 %all-to-all-start.2 = ((bf16[8,16,512]{2,1,0:T(8,128)(2,1)}), bf16[8,16,512]{2,1,0:T(8,128)(2,1)S(1)}, u32[]{:S(2)}, u32[]{:S(2)}) async-start(bf16[8,16,512]{2,1,0:T(8,128)(2,1)} %bitcast.8), calls=%async_computation.2 | async-start | bytes 262144 | tf_op jit(solution)/shard_map/all_to_all | solution.py:58
  31.4 3.8 %copy.78 = bf16[1,16,4096]{1,0,2:T(2,128)(2,1)} copy(bf16[1,16,4096]{2,1,0:T(8,128)(2,1)S(1)} %bitcast.109) | data formatting | bytes 262144 | tf_op jit(solution)/shard_map/all_to_all | solution.py:51
  35.2 0.6 broadcast.52
  35.8 23.4 %reduce.3 = bf16[4096,16]{1,0:T(8,128)(2,1)S(1)} reduce(bf16[4096,1,16]{2,1,0:T(2,128)(2,1)} %bitcast.95, bf16[]{:T(256)} %broadcast.52), dimensions={1}, to_apply=%bitcast.68.reduce_sub_computation | reduce | bytes 262146
  59.3 1.7 reshape.72
  61.0 3.7 %all-to-all-start.1 = ((bf16[4,2,8192]{2,1,0:T(2,128)(2,1)}), bf16[4,2,8192]{2,1,0:T(2,128)(2,1)S(1)}, u32[]{:S(2)}, u32[]{:S(2)}) async-start(bf16[4,2,8192]{2,1,0:T(2,128)(2,1)} %reshape.72), calls=%async_computation.1 | async-start | bytes 262144 | tf_op jit(solution)/shard_map/all_to_all | solution.py:50
  64.7 3.8 %copy.82 = bf16[1,16,4096]{1,0,2:T(2,128)(2,1)} copy(bf16[1,16,4096]{2,1,0:T(8,128)(2,1)S(1)} %bitcast.110) | data formatting | bytes 262144 | tf_op jit(solution)/shard_map/all_to_all | solution.py:58
  68.5 23.4 %reduce.2 = bf16[4096,16]{1,0:T(8,128)(2,1)S(1)} reduce(bf16[4096,1,16]{2,1,0:T(2,128)(2,1)} %bitcast.97, bf16[]{:T(256)} %broadcast.52), dimensions={1}, to_apply=%bitcast.66.reduce_sub_computation | reduce | bytes 262146
  91.9 1.7 reshape.70
  93.7 4.2 %all-to-all-start.3 = ((bf16[4,2,8192]{2,1,0:T(2,128)(2,1)}), bf16[4,2,8192]{2,1,0:T(2,128)(2,1)S(1)}, u32[]{:S(2)}, u32[]{:S(2)}) async-start(bf16[4,2,8192]{2,1,0:T(2,128)(2,1)} %reshape.70), calls=%async_computation.3 | async-start | bytes 262144 | tf_op jit(solution)/shard_map/all_to_all | solution.py:57
  97.9 2.7 %reshape.73 = bf16[4096,1,16]{2,1,0:T(2,128)(2,1)} reshape(bf16[4,2,8192]{2,1,0:T(2,128)(2,1)S(1)} %all-to-all-done.1) | data formatting | bytes 262144
  100.6 4.4 %copy.79 = bf16[1,16,4096]{2,1,0:T(8,128)(2,1)S(1)} copy(bf16[1,16,4096]{1,0,2:T(2,128)(2,1)} %bitcast.98) | data formatting | bytes 262144 | tf_op jit(solution)/shard_map/all_to_all | solution.py:50
  105.1 0.5 fusion.4
  105.6 1.0 copy-done.1
  106.7 0.5 fusion.8
  107.2 2.7 %reshape.71 = bf16[4096,1,16]{2,1,0:T(2,128)(2,1)} reshape(bf16[4,2,8192]{2,1,0:T(2,128)(2,1)S(1)} %all-to-all-done.3) | data formatting | bytes 262144
  109.9 4.4 %copy.83 = bf16[1,16,4096]{2,1,0:T(8,128)(2,1)S(1)} copy(bf16[1,16,4096]{1,0,2:T(2,128)(2,1)} %bitcast.99) | data formatting | bytes 262144 | tf_op jit(solution)/shard_map/all_to_all | solution.py:57
  114.5 2.4 fusion
  116.8 0.9 pad_maximum_fusion
  117.8 0.1 copy.76
  117.9 0.1 broadcast_in_dim.38
  118.0 0.3 select_reduce_fusion
  118.3 0.1 dynamic_slice.3
  118.4 27.5 %reduce-scatter.2.cloned.1.call-done = f32[16,3072]{1,0:T(8,128)} async-done(((f32[64,3072]{1,0:T(8,128)}), f32[16,3072]{1,0:T(8,128)}) %reduce-scatter.2.cloned.1.call-update) | async-done | bytes 196624 | tf_op jit(solution)/shard_map/reduce_scatter | solution.py:72
  145.9 1.1 multiply_convert_fusion
  147.1 9.0 %all_gather.11 = bf16[64,1024]{1,0:T(8,128)(2,1)} all-gather(bf16[16,1024]{1,0:T(8,128)(2,1)S(1)} %get-tuple-element.8), channel_id=1, replica_groups=mesh['ep'=4,'edp'=8] {'ep'}, dimensions={0}, use_global_device_ids=true | all-gather | bytes 163840 | tf_op jit(solution)/shard_map/all_gather | solution.py:96
  156.1 7.6 %all_gather.9 = bf16[64,1024]{1,0:T(8,128)(2,1)S(1)} all-gather(bf16[16,1024]{1,0:T(8,128)(2,1)S(1)} %get-tuple-element.9), channel_id=1, replica_groups=mesh['ep'=4,'edp'=8] {'ep'}, dimensions={0}, use_global_device_ids=true | all-gather | bytes 163840 | tf_op jit(solution)/shard_map/all_gather | solution.py:94
  163.6 8.7 %all_gather.10 = bf16[64,1024]{1,0:T(8,128)(2,1)S(1)} all-gather(bf16[16,1024]{1,0:T(8,128)(2,1)S(1)} %get-tuple-element.10), channel_id=1, replica_groups=mesh['ep'=4,'edp'=8] {'ep'}, dimensions={0}, use_global_device_ids=true | all-gather | bytes 163840 | tf_op jit(solution)/shard_map/all_gather | solution.py:95
  172.3 0.8 fusion.2
  173.1 0.8 fusion.16
  173.8 0.2 copy.98
  174.1 1.4 reduce.4
  175.4 0.7 reshape.74
  176.1 3.3 %all-to-all-start.4 = ((bf16[4,2,8192]{2,1,0:T(2,128)(2,1)}), bf16[4,2,8192]{2,1,0:T(2,128)(2,1)S(1)}, u32[]{:S(2)}, u32[]{:S(2)}) async-start(bf16[4,2,8192]{2,1,0:T(2,128)(2,1)} %reshape.74), calls=%async_computation.5 | async-start | bytes 262144 | tf_op jit(solution)/shard_map/all_to_all | solution.py:113
  179.5 2.1 convert_bitcast_fusion.2
  181.5 2.9 %all-to-all-done.4 = bf16[4,2,8192]{2,1,0:T(2,128)(2,1)S(1)} async-done(((bf16[4,2,8192]{2,1,0:T(2,128)(2,1)}), bf16[4,2,8192]{2,1,0:T(2,128)(2,1)S(1)}, u32[]{:S(2)}, u32[]{:S(2)}) %all-to-all-start.4) | async-done | bytes 131104 | tf_op jit(solution)/shard_map/all_to_all | solution.py:113
  184.5 0.1 reshape.75
  184.7 3.8 %copy.87 = bf16[1,16,4096]{1,0,2:T(2,128)(2,1)} copy(bf16[1,16,4096]{2,1,0:T(8,128)(2,1)S(1)} %bitcast.112) | data formatting | bytes 262144 | tf_op jit(solution)/shard_map/all_to_all | solution.py:113
  188.5 23.4 %reduce.5 = bf16[4096,16]{1,0:T(8,128)(2,1)S(1)} reduce(bf16[4096,1,16]{2,1,0:T(2,128)(2,1)} %bitcast.96, bf16[]{:T(256)} %broadcast.52), dimensions={1}, to_apply=%bitcast.72.reduce_sub_computation | reduce | bytes 262146
  211.9 1.7 reshape.76
  213.6 4.7 %all-to-all-start.5 = ((bf16[8,2,4096]{2,1,0:T(2,128)(2,1)}), bf16[8,2,4096]{2,1,0:T(2,128)(2,1)S(1)}, u32[]{:S(2)}, u32[]{:S(2)}) async-start(bf16[8,2,4096]{2,1,0:T(2,128)(2,1)} %reshape.76), calls=%async_computation.6 | async-start | bytes 262144 | tf_op jit(solution)/shard_map/all_to_all | solution.py:112
  218.3 2.1 convert_bitcast_fusion.1
  220.4 2.1 convert_bitcast_fusion
  222.5 2.7 %all-to-all-done.5 = bf16[8,2,4096]{2,1,0:T(2,128)(2,1)S(1)} async-done(((bf16[8,2,4096]{2,1,0:T(2,128)(2,1)}), bf16[8,2,4096]{2,1,0:T(2,128)(2,1)S(1)}, u32[]{:S(2)}, u32[]{:S(2)}) %all-to-all-start.5) | async-done | bytes 131104 | tf_op jit(solution)/shard_map/all_to_all | solution.py:112
  225.1 3.9 %reshape.77 = bf16[4096,1,16]{2,1,0:T(2,128)(2,1)} reshape(bf16[8,2,4096]{2,1,0:T(2,128)(2,1)S(1)} %all-to-all-done.5) | data formatting | bytes 262144
  229.1 4.4 %copy.88 = bf16[1,16,4096]{2,1,0:T(8,128)(2,1)S(1)} copy(bf16[1,16,4096]{1,0,2:T(2,128)(2,1)} %bitcast.100) | data formatting | bytes 262144 | tf_op jit(solution)/shard_map/all_to_all | solution.py:112
  233.6 0.8 convolution_convert_fusion
  (31 shorter events, 0.6 us)
Async XLA Ops:
  7.2 98.0 %copy-start = (bf16[1,1024,1024]{2,1,0:T(8,128)(2,1)S(1)}, bf16[1,1024,1024]{2,1,0:T(8,128)(2,1)}, u32[]{:S(2)}) copy-start(bf16[1,1024,1024]{2,1,0:T(8,128)(2,1)} %param.12) | copy-start | bytes 6291460
  14.9 13.1 %all-to-all-start = ((bf16[8,16,512]{2,1,0:T(8,128)(2,1)}), bf16[8,16,512]{2,1,0:T(8,128)(2,1)S(1)}, u32[]{:S(2)}, u32[]{:S(2)}) async-start(bf16[8,16,512]{2,1,0:T(8,128)(2,1)} %bitcast.1), calls=%async_computation | async-start | bytes 262144 | tf_op jit(solution)/shard_map/all_to_all | solution.py:51
  28.0 32.9 %all-to-all-start.2 = ((bf16[8,16,512]{2,1,0:T(8,128)(2,1)}), bf16[8,16,512]{2,1,0:T(8,128)(2,1)S(1)}, u32[]{:S(2)}, u32[]{:S(2)}) async-start(bf16[8,16,512]{2,1,0:T(8,128)(2,1)} %bitcast.8), calls=%async_computation.2 | async-start | bytes 262144 | tf_op jit(solution)/shard_map/all_to_all | solution.py:58
  61.0 32.7 %all-to-all-start.1 = ((bf16[4,2,8192]{2,1,0:T(2,128)(2,1)}), bf16[4,2,8192]{2,1,0:T(2,128)(2,1)S(1)}, u32[]{:S(2)}, u32[]{:S(2)}) async-start(bf16[4,2,8192]{2,1,0:T(2,128)(2,1)} %reshape.72), calls=%async_computation.1 | async-start | bytes 262144 | tf_op jit(solution)/shard_map/all_to_all | solution.py:50
  93.7 13.5 %all-to-all-start.3 = ((bf16[4,2,8192]{2,1,0:T(2,128)(2,1)}), bf16[4,2,8192]{2,1,0:T(2,128)(2,1)S(1)}, u32[]{:S(2)}, u32[]{:S(2)}) async-start(bf16[4,2,8192]{2,1,0:T(2,128)(2,1)} %reshape.70), calls=%async_computation.3 | async-start | bytes 262144 | tf_op jit(solution)/shard_map/all_to_all | solution.py:57
  97.9 48.1 %reduce-scatter.2.cloned.1.call-start = ((), (), s32[]{:S(2)}) async-start(), calls=%async_computation.7 | async-start | bytes 983040 | tf_op jit(solution)/shard_map/reduce_scatter | solution.py:72
  105.1 1.6 copy-start.1
  114.4 3.3 %copy-start.5 = (f32[128,8]{0,1:T(8,128)S(1)}, f32[128,8]{0,1:T(8,128)}, u32[]{:S(2)}) copy-start(f32[128,8]{0,1:T(8,128)} %param.9) | copy-start | bytes 12292
  114.5 3.5 %copy-start.4 = (s32[1024]{0:T(1024)S(1)}, s32[1024]{0:T(1024)}, u32[]{:S(2)}) copy-start(s32[1024]{0:T(1024)} %get-tuple-element.6) | copy-start | bytes 12292
  145.9 27.1 %copy-start.2 = (bf16[1,1024,1024]{2,1,0:T(8,128)(2,1)S(1)}, bf16[1,1024,1024]{2,1,0:T(8,128)(2,1)}, u32[]{:S(2)}) copy-start(bf16[1,1024,1024]{2,1,0:T(8,128)(2,1)} %param.11) | copy-start | bytes 6291460
  176.1 8.3 %all-to-all-start.4 = ((bf16[4,2,8192]{2,1,0:T(2,128)(2,1)}), bf16[4,2,8192]{2,1,0:T(2,128)(2,1)S(1)}, u32[]{:S(2)}, u32[]{:S(2)}) async-start(bf16[4,2,8192]{2,1,0:T(2,128)(2,1)} %reshape.74), calls=%async_computation.5 | async-start | bytes 262144 | tf_op jit(solution)/shard_map/all_to_all | solution.py:113
  213.6 6.8 %copy-start.3 = (bf16[64,1024]{1,0:T(8,128)(2,1)S(1)}, bf16[64,1024]{1,0:T(8,128)(2,1)}, u32[]{:S(2)}) copy-start(bf16[64,1024]{1,0:T(8,128)(2,1)} %all_gather.11) | copy-start | bytes 393220
  213.6 11.5 %all-to-all-start.5 = ((bf16[8,2,4096]{2,1,0:T(2,128)(2,1)}), bf16[8,2,4096]{2,1,0:T(2,128)(2,1)S(1)}, u32[]{:S(2)}, u32[]{:S(2)}) async-start(bf16[8,2,4096]{2,1,0:T(2,128)(2,1)} %reshape.76), calls=%async_computation.6 | async-start | bytes 262144 | tf_op jit(solution)/shard_map/all_to_all | solution.py:112
Sparse Core Ops, SparseCore 0:
  117.9 27.9 reduce-scatter.1
where the time goes:
time: 243 us; the launch traced here: 241 us
  other arithmetic  78.2 us (32%)
  local copies, waits for them, and re-layouts  44.4 us (18%)
  waiting for transfers between devices  38.1 us (16%)
  starting transfers between devices  25.7 us (11%)
  blocking collectives  25.2 us (10%)
  matrix products  15.4 us (6%)
  between operations  14.3 us (6%)
    unnamed x5, other arithmetic  71.7 us
    reduce_scatter x1, waiting for transfers between devices, per_device(): lax.psum_scatter(jnp.concatenate([jnp.dot(slot_tokens, gate_local, prefer...  27.5 us
    unnamed x25, local copies, waits for them, and re-layouts  18.1 us
    all_gather x1, blocking collectives, per_device(): lax.all_gather(hidden_weighted, 'ep', axis=0, tiled=True)  8.99 us
    all_gather x1, blocking collectives, per_device(): lax.all_gather(up_grad, 'ep', axis=0, tiled=True)  8.67 us
    all_gather x1, blocking collectives, per_device(): lax.all_gather(gate_grad, 'ep', axis=0, tiled=True)  7.56 us
    all_to_all x1, starting transfers between devices, per_device(): lax.all_to_all(tok_block, 'edp', split_axis=0, concat_axis=2, tiled=True)  6.32 us
    all_to_all x1, waiting for transfers between devices, per_device(): lax.all_to_all(tok_block, 'edp', split_axis=0, concat_axis=2, tiled=True)  4.99 us
  transfers between devices with their start and end apart: 7, of which 4 were waited for; matrix products, arithmetic and copies ran while one was open for 31% of the time, Pallas kernels for 0%

commit v1 on v0

v1 whole, which is shorter than its diff:
```python
import functools

import jax
import jax.numpy as jnp
from jax import lax
from jax.experimental import pallas as pl
from jax.experimental.pallas import tpu as pltpu
from jax.sharding import PartitionSpec as P

CAP = 16
MESH = pl.DeviceIdType.MESH
SUM_TYPE = jnp.float32
CONTRACT_FIRST = (((0,), (0,)), ((), ()))
CONTRACT_LAST = (((1,), (1,)), ((), ()))


def dot_f32(a, b, dims=(((1,), (0,)), ((), ()))):
    return lax.dot_general(a, b, dims, preferred_element_type=jnp.float32)


def remote(src, dst, send_sem, recv_sem, device):
    return pltpu.make_async_remote_copy(
        src_ref=src,
        dst_ref=dst,
        send_sem=send_sem,
        recv_sem=recv_sem,
        device_id=device,
        device_id_type=MESH,
    )


def steps(count, body):
    if count <= 8:
        for k in range(count):
            body(k)
    else:
        lax.fori_loop(0, count, lambda k, c: (body(k), c)[1], 0)


def exchange_kernel(
    ep,
    edp,
    tok_ref,
    grad_ref,
    probs_ref,
    ids_ref,
    wg_hbm,
    wu_hbm,
    wd_hbm,
    disp_out,
    ret_out,
    x_out,
    y_out,
    gg_out,
    ug_out,
    hw_out,
    wg,
    wu,
    wd,
    disp_t,
    pick_w,
    send_t,
    send_y,
    recv_t,
    recv_y,
    part,
    send_p,
    recv_p,
    hid,
    send_s,
    ret,
    w_sem,
    ss_t,
    rs_t,
    ss_y,
    rs_y,
    ss_p,
    rs_p,
    ss_h,
    rs_h,
    ss_r,
    rs_r,
):
    me_i = lax.axis_index("ep")
    me_j = lax.axis_index("edp")
    per = edp // ep
    home = me_j // per
    my_part = lax.rem(me_j, per)
    tok_rows, feat = tok_ref.shape
    slots = edp * CAP
    mine = pl.ds(pl.multiple_of(me_i * CAP, CAP), CAP)
    at_home = home == me_i

    loads = [
        pltpu.make_async_copy(src.at[0], dst, w_sem.at[n])
        for n, (src, dst) in enumerate(((wg_hbm, wg), (wu_hbm, wu), (wd_hbm, wd)))
    ]
    for load in loads:
        load.start()

    barrier = pltpu.get_barrier_semaphore()

    def greet(device):
        pl.semaphore_signal(barrier, inc=1, device_id=device, device_id_type=MESH)

    def greet_experts(k):
        e = lax.rem(me_j + 1 + k, edp)

        @pl.when(jnp.logical_not(jnp.logical_and(at_home, e == me_j)))
        def _():
            greet((home, e))

    def greet_owners(k):
        i = lax.rem(me_i + k // per, ep)
        j = me_i * per + lax.rem(k, per)

        @pl.when(jnp.logical_not(jnp.logical_and(i == me_i, j == me_j)))
        def _():
            greet((i, j))

    steps(edp, greet_experts)
    steps(edp, greet_owners)
    for d in range(1, ep):
        greet((lax.rem(me_i + d, ep), me_j))

    lane = lax.broadcasted_iota(jnp.int32, (tok_rows, slots), 1)
    expert = lax.shift_right_logical(lane, 4)
    place = lax.bitwise_and(lane, CAP - 1).astype(jnp.float32)
    chosen = jnp.zeros((tok_rows, slots), jnp.float32)
    weight = jnp.zeros((tok_rows, slots), jnp.float32)
    for k in range(ids_ref.shape[1]):
        hit = ids_ref[:, k : k + 1] == expert
        chosen = jnp.where(hit, 1.0, chosen)
        weight = jnp.where(hit, probs_ref[:, k : k + 1], weight)
    row = lax.broadcasted_iota(jnp.int32, (tok_rows, tok_rows), 0)
    col = lax.broadcasted_iota(jnp.int32, (tok_rows, tok_rows), 1)
    before = jnp.where(col < row, 1.0, 0.0).astype(jnp.bfloat16)
    rank = dot_f32(before, chosen.astype(jnp.bfloat16))
    disp = jnp.where(rank == place, chosen, 0.0)
    disp_out[...] = disp.astype(jnp.bfloat16)
    disp_t[...] = disp.T.astype(jnp.bfloat16)
    pick_w[...] = (disp * weight).T
    send_t[...] = dot_f32(disp_t[...], tok_ref[...]).astype(jnp.bfloat16)

    @pl.when(at_home)
    def _():
        pl.semaphore_wait(barrier, 2 * edp + ep - 1 - 2)

    @pl.when(jnp.logical_not(at_home))
    def _():
        pl.semaphore_wait(barrier, 2 * edp + ep - 1)

    def dispatch(k, send, recv, send_sem, recv_sem, action):
        e = lax.rem(me_j + 1 + k, edp)
        here = jnp.logical_and(at_home, e == me_j)
        src = send.at[pl.ds(pl.multiple_of(e * CAP, CAP), CAP), :]
        dst = recv.at[my_part, mine, :]
        arrive = recv_sem.at[my_part, me_i]

        @pl.when(here)
        def _():
            if action == "start":
                pltpu.make_async_copy(src, dst, arrive).start()

        @pl.when(jnp.logical_not(here))
        def _():
            copy = remote(src, dst, send_sem.at[e], arrive, (home, e))
            if action == "start":
                copy.start()
            else:
                copy.wait_send()

    def landed(k, recv, recv_sem):
        i = k // per
        p = lax.rem(k, per)
        spot = recv.at[p, pl.ds(pl.multiple_of(i * CAP, CAP), CAP), :]
        pltpu.make_async_copy(spot, spot, recv_sem.at[p, i]).wait()

    steps(edp, lambda k: dispatch(k, send_t, recv_t, ss_t, rs_t, "start"))
    send_y[...] = dot_f32(disp_t[...], grad_ref[...]).astype(jnp.bfloat16)
    steps(edp, lambda k: dispatch(k, send_y, recv_y, ss_y, rs_y, "start"))

    def share_sum(m, total):
        part[m, :, :] = total
        if send_p is not part:
            send_p[m, :, :] = total.astype(SUM_TYPE)
        for d in range(1, ep):
            sum_copy(m, d).start()

    def sum_copy(m, d):
        to = lax.rem(me_i + d, ep)
        src = send_p.at[m, pl.ds(pl.multiple_of(to * CAP, CAP), CAP), :]
        return remote(
            src, recv_p.at[m, d - 1], ss_p.at[m, d - 1], rs_p.at[m, d - 1], (to, me_j)
        )

    def gathered_sum(m):
        total = part[m, mine, :]
        for d in range(1, ep):
            sum_copy(m, d).wait_recv()
            total = total + recv_p[m, d - 1, :, :].astype(jnp.float32)
        return total

    loads[0].wait()
    steps(edp, lambda k: landed(k, recv_t, rs_t))
    for p in range(per):
        x_out[:, p * feat : (p + 1) * feat] = recv_t[p, :, :]
    share_sum(0, dot_f32(x_out[...], wg[...]))
    loads[1].wait()
    share_sum(1, dot_f32(x_out[...], wu[...]))
    loads[2].wait()
    steps(edp, lambda k: landed(k, recv_y, rs_y))
    for p in range(per):
        y_out[:, p * feat : (p + 1) * feat] = recv_y[p, :, :]
    share_sum(2, dot_f32(y_out[...], wd[...], CONTRACT_LAST))

    own = pl.ds(pl.multiple_of(me_j * CAP, CAP), CAP)
    weight_col = jnp.sum(pick_w[own, :], axis=1, keepdims=True)

    def hid_copy(m, d):
        spot = hid.at[m, mine, :]
        return remote(
            spot, spot, ss_h.at[m, d - 1], rs_h.at[m, d - 1], (lax.rem(me_i + d, ep), me_j)
        )

    def hid_arrived(m):
        for d in range(1, ep):
            came = lax.rem(me_i + ep - d, ep)
            spot = hid.at[m, pl.ds(pl.multiple_of(came * CAP, CAP), CAP), :]
            pltpu.make_async_copy(spot, spot, rs_h.at[m, d - 1]).wait()

    def share_hidden(m, value):
        hid[m, mine, :] = value.astype(jnp.bfloat16)
        for d in range(1, ep):
            hid_copy(m, d).start()

    gate_sum = gathered_sum(0)
    up_sum = gathered_sum(1)
    sig = jax.nn.sigmoid(gate_sum)
    silu = gate_sum * sig
    slope = up_sum * sig * (1.0 + gate_sum * (1.0 - sig))
    hidden_grad = weight_col * gathered_sum(2)
    share_hidden(0, hidden_grad * slope)
    share_hidden(1, hidden_grad * silu)
    share_hidden(2, weight_col * silu * up_sum)

    hid_arrived(0)
    slot_grad = dot_f32(hid[0, :, :], wg[...], CONTRACT_LAST)
    hid_arrived(1)
    slot_grad = (slot_grad + dot_f32(hid[1, :, :], wu[...], CONTRACT_LAST)).astype(jnp.bfloat16)
    for p in range(per):
        send_s[p, :, :] = slot_grad[:, p * feat : (p + 1) * feat]

    def give_back(k, action):
        i = lax.rem(me_i + 1 + k // per, ep)
        p = lax.rem(k, per)
        j = me_i * per + p
        here = jnp.logical_and(i == me_i, j == me_j)
        src = send_s.at[p, pl.ds(pl.multiple_of(i * CAP, CAP), CAP), :]
        dst = ret.at[own, :]

        @pl.when(here)
        def _():
            if action == "start":
                pltpu.make_async_copy(src, dst, rs_r.at[me_j]).start()

        @pl.when(jnp.logical_not(here))
        def _():
            copy = remote(src, dst, ss_r.at[p, i], rs_r.at[me_j], (i, j))
            if action == "start":
                copy.start()
            else:
                copy.wait_send()

    def returned(e):
        spot = ret.at[pl.ds(pl.multiple_of(e * CAP, CAP), CAP), :]
        pltpu.make_async_copy(spot, spot, rs_r.at[e]).wait()

    steps(edp, lambda k: give_back(k, "start"))
    gg_out[...] = hid[0, :, :]
    ug_out[...] = hid[1, :, :]
    hid_arrived(2)
    hw_out[...] = hid[2, :, :]
    steps(edp, lambda k: dispatch(k, send_t, recv_t, ss_t, rs_t, "wait"))
    steps(edp, lambda k: dispatch(k, send_y, recv_y, ss_y, rs_y, "wait"))
    for m in range(3):
        for d in range(1, ep):
            sum_copy(m, d).wait_send()
            hid_copy(m, d).wait_send()
    steps(edp, returned)
    ret_out[...] = ret[...]
    steps(edp, lambda k: give_back(k, "wait"))


def grads_kernel(
    disp_ref, ret_ref, x_ref, y_ref, gg_ref, ug_ref, hw_ref, tg_ref, dg_ref, du_ref, dd_ref
):
    dg_ref[0, :, :] = dot_f32(x_ref[...], gg_ref[...], CONTRACT_FIRST).astype(jnp.bfloat16)
    du_ref[0, :, :] = dot_f32(x_ref[...], ug_ref[...], CONTRACT_FIRST).astype(jnp.bfloat16)
    dd_ref[0, :, :] = dot_f32(hw_ref[...], y_ref[...], CONTRACT_FIRST).astype(jnp.bfloat16)
    tg_ref[...] = dot_f32(disp_ref[...], ret_ref[...]).astype(jnp.bfloat16)


def per_device(tokens, out_grad, probs, expert_ids, w_gate, w_up, w_down):
    ep, edp = lax.axis_size("ep"), lax.axis_size("edp")
    per = edp // ep
    tok_rows, feat = tokens.shape
    width, hidden = w_gate.shape[1:]
    slots = edp * CAP
    rows = ep * CAP
    bf16, f32 = jnp.bfloat16, jnp.float32
    vmem = pl.BlockSpec(memory_space=pltpu.VMEM)
    anywhere = pl.BlockSpec(memory_space=pl.ANY)
    dma = pltpu.SemaphoreType.DMA
    disp, ret, x_s, y_s, gg, ug, hw = pl.pallas_call(
        functools.partial(exchange_kernel, ep, edp),
        out_shape=[
            jax.ShapeDtypeStruct((tok_rows, slots), bf16),
            jax.ShapeDtypeStruct((slots, feat), bf16),
            jax.ShapeDtypeStruct((rows, width), bf16),
            jax.ShapeDtypeStruct((rows, width), bf16),
            jax.ShapeDtypeStruct((rows, hidden), bf16),
            jax.ShapeDtypeStruct((rows, hidden), bf16),
            jax.ShapeDtypeStruct((rows, hidden), bf16),
        ],
        in_specs=[vmem] * 4 + [anywhere] * 3,
        out_specs=[vmem] * 7,
        scratch_shapes=[
            pltpu.VMEM((width, hidden), bf16),
            pltpu.VMEM((width, hidden), bf16),
            pltpu.VMEM((hidden, width), bf16),
            pltpu.VMEM((slots, tok_rows), bf16),
            pltpu.VMEM((slots, tok_rows), f32),
            pltpu.VMEM((slots, feat), bf16),
            pltpu.VMEM((slots, feat), bf16),
            pltpu.VMEM((per, rows, feat), bf16),
            pltpu.VMEM((per, rows, feat), bf16),
            pltpu.VMEM((3, rows, hidden), f32),
            pltpu.VMEM((3, rows, hidden), SUM_TYPE),
            pltpu.VMEM((3, ep - 1, CAP, hidden), SUM_TYPE),
            pltpu.VMEM((3, rows, hidden), bf16),
            pltpu.VMEM((per, rows, feat), bf16),
            pltpu.VMEM((slots, feat), bf16),
            dma((3,)),
            dma((edp,)),
            dma((per, ep)),
            dma((edp,)),
            dma((per, ep)),
            dma((3, ep - 1)),
            dma((3, ep - 1)),
            dma((3, ep - 1)),
            dma((3, ep - 1)),
            dma((per, ep)),
            dma((edp,)),
        ],
        compiler_params=pltpu.CompilerParams(
            collective_id=0, has_side_effects=True, vmem_limit_bytes=48 * 1024 * 1024
        ),
        cost_estimate=pl.CostEstimate(
            flops=10 * rows * width * hidden,
            bytes_accessed=6 * width * hidden,
            transcendentals=CAP * hidden,
        ),
    )(tokens, out_grad, probs, expert_ids, w_gate, w_up, w_down)

    tiles = max(1, min(4, width // 128))

    def whole(shape):
        return pl.BlockSpec(shape, lambda n: (0, 0))

    token_grad, grad_gate, grad_up, grad_down = pl.pallas_call(
        grads_kernel,
        grid=(tiles,),
        out_shape=[
            jax.ShapeDtypeStruct((tok_rows, feat), bf16),
            jax.ShapeDtypeStruct((1, width, hidden), bf16),
            jax.ShapeDtypeStruct((1, width, hidden), bf16),
            jax.ShapeDtypeStruct((1, hidden, width), bf16),
        ],
        in_specs=[
            pl.BlockSpec((tok_rows // tiles, slots), lambda n: (n, 0)),
            whole((slots, feat)),
            pl.BlockSpec((rows, width // tiles), lambda n: (0, n)),
            whole((rows, width)),
            whole((rows, hidden)),
            whole((rows, hidden)),
            pl.BlockSpec((rows, hidden // tiles), lambda n: (0, n)),
        ],
        out_specs=[
            pl.BlockSpec((tok_rows // tiles, feat), lambda n: (n, 0)),
            pl.BlockSpec((1, width // tiles, hidden), lambda n: (0, n, 0)),
            pl.BlockSpec((1, width // tiles, hidden), lambda n: (0, n, 0)),
            pl.BlockSpec((1, hidden // tiles, width), lambda n: (0, n, 0)),
        ],
        compiler_params=pltpu.CompilerParams(vmem_limit_bytes=32 * 1024 * 1024),
        cost_estimate=pl.CostEstimate(
            flops=6 * rows * width * hidden,
            bytes_accessed=6 * width * hidden,
            transcendentals=0,
        ),
    )(disp, ret, x_s, y_s, gg, ug, hw)
    return token_grad, grad_gate, grad_up, grad_down


def solution(mesh):
    placed = (
        P("ep", "edp"),
        P("ep", "edp"),
        P("ep", None),
        P("ep", None),
        P("edp", "ep", None),
        P("edp", "ep", None),
        P("edp", None, "ep"),
    )
    return jax.shard_map(
        per_device,
        mesh=mesh,
        in_specs=placed,
        out_specs=(
            P("ep", "edp"),
            P("edp", "ep", None),
            P("edp", "ep", None),
            P("edp", None, "ep"),
        ),
        check_vma=False,
    )
```

time: 243 us -> 50.9 us (0.21)
  other arithmetic: 78.2 us -> 0 us
  Pallas kernels: 0 us -> 43.4 us
  waiting for transfers between devices: 38.1 us -> 0 us
  local copies, waits for them, and re-layouts: 44.4 us -> 6.56 us
  starting transfers between devices: 25.7 us -> 0 us
  blocking collectives: 25.2 us -> 0 us
  matrix products: 15.4 us -> 0 us
  between operations: 14.3 us -> 0.65 us
    unnamed x5 -> x0, other arithmetic: 71.7 us -> none
    pallas_call x0 -> x2, Pallas kernels: none -> 43.4 us  [the longest x1 39.5 us: per_device(): pl.pallas_call(functools.partial(exchange_kernel, ep, edp), out_shape=[ja...]
    reduce_scatter x1 -> x0, waiting for transfers between devices: 27.5 us -> none  [per_device(): lax.psum_scatter(jnp.concatenate([jnp.dot(slot_tokens, gate_local, prefer...]
    all_to_all x6 -> x0, starting transfers between devices: 25.7 us -> none  [the longest x1 6.32 us: per_device(): lax.all_to_all(tok_block, 'edp', split_axis=0, concat_axis=2, tiled=True)]
    all_gather x3 -> x0, blocking collectives: 25.2 us -> none  [the longest x1 8.99 us: per_device(): lax.all_gather(hidden_weighted, 'ep', axis=0, tiled=True)]
    all_to_all x15 -> x0, local copies, waits for them, and re-layouts: 25 us -> none  [the longest x3 4.53 us: per_device(): lax.all_to_all(lax.all_to_all(grad_block, 'edp', split_axis=0, concat_axi...]
    dot_general x11 -> x0, matrix products: 15.4 us -> none  [the longest x1 2.35 us: per_device(): lax.dot_general(slot_grads, down_local, contract_last, preferred_element_...]
    unnamed x25 -> x10, local copies, waits for them, and re-layouts: 18.1 us -> 6.56 us
  transfers between devices with their start and end apart: 7 -> 0, of which waited for: 4 -> 0; matrix products, arithmetic and copies ran while one was open for 31% -> 0% of each run, Pallas kernels for 0% -> 0%
where the time goes in v1:
time: 50.9 us; the launch traced here: 50.6 us
  Pallas kernels  43.4 us (85%)
  local copies, waits for them, and re-layouts  6.56 us (13%)
  between operations  0.65 us (1%)
    pallas_call x1, Pallas kernels, per_device(): pl.pallas_call(functools.partial(exchange_kernel, ep, edp), out_shape=[ja...  39.5 us
    unnamed x10, local copies, waits for them, and re-layouts  6.56 us
    pallas_call x1, Pallas kernels, per_device(): pl.pallas_call(grads_kernel, grid=(tiles,), out_shape=[jax.ShapeDtypeStru...  3.89 us

profile of v1, /device:TPU:0, one launch (start us, length us, event | category | flops | bytes accessed | tf_op | source)
XLA Modules:
  0.0 50.6 jit_solution(7618979242357864435)
XLA Ops:
  0.6 0.8 %copy.11.probs_ref = f32[128,8]{1,0:T(8,128)S(1)} copy(f32[128,8]{0,1:T(8,128)} %param.9) | data formatting | bytes 8192 | tf_op args[2]
  1.4 0.8 %copy.12.ids_ref = s32[128,8]{1,0:T(8,128)S(1)} copy(s32[128,8]{0,1:T(8,128)} %param.10) | data formatting | bytes 8192 | tf_op args[3]
  2.2 0.0 copy-start
  2.2 1.6 %copy-done = bf16[1,1024,1024]{2,1,0:T(8,128)(2,1)S(1)} copy-done((bf16[1,1024,1024]{2,1,0:T(8,128)(2,1)S(1)}, bf16[1,1024,1024]{2,1,0:T(8,128)(2,1)}, u32[]{:S(2)}) %copy-start) | copy-done | bytes 2097176
  3.8 0.0 copy-start.1
  3.8 1.6 %copy-done.1 = bf16[1,1024,1024]{2,1,0:T(8,128)(2,1)S(1)} copy-done((bf16[1,1024,1024]{2,1,0:T(8,128)(2,1)S(1)}, bf16[1,1024,1024]{2,1,0:T(8,128)(2,1)}, u32[]{:S(2)}) %copy-start.1) | copy-done | bytes 2097176
  5.4 0.0 copy-start.2
  5.4 0.9 %copy-done.2 = bf16[128,512]{1,0:T(8,128)(2,1)S(1)} copy-done((bf16[128,512]{1,0:T(8,128)(2,1)S(1)}, bf16[128,512]{1,0:T(8,128)(2,1)}, u32[]{:S(2)}) %copy-start.2) | copy-done | bytes 131096
  6.3 0.0 copy-start.3
  6.3 0.9 %copy-done.3 = bf16[128,512]{1,0:T(8,128)(2,1)S(1)} copy-done((bf16[128,512]{1,0:T(8,128)(2,1)S(1)}, bf16[128,512]{1,0:T(8,128)(2,1)}, u32[]{:S(2)}) %copy-start.3) | copy-done | bytes 131096
  7.2 39.5 %shard_map.102 = (bf16[128,128]{1,0:T(8,128)(2,1)S(1)}, bf16[128,512]{1,0:T(8,128)(2,1)S(1)}, bf16[64,1024]{1,0:T(8,128)(2,1)S(1)}, bf16[64,1024]{1,0:T(8,128)(2...) custom-call(bf16[128,512]{1,0:T(8,128)(2,1)S(1)} %copy-done.2, ...), custom_call_target="tpu_custom_call" | custom-call | flops 671088640 | bytes 6291456 | tf_op jit(solution)/shard_map/pallas_call | solution.py:315
  46.7 3.9 %shard_map.103 = (bf16[128,512]{1,0:T(8,128)(2,1)}, bf16[1,1024,1024]{2,1,0:T(8,128)(2,1)}, bf16[1,1024,1024]{2,1,0:T(8,128)(2,1)}, bf16[1,1024,1024]{2,1,0:T(8,128)(2,1)}) custom-call(bf16[128,128]{1,0:T(8,128)(2,1)S(1)} %get-tuple-element.11.disp_ref, bf16[128,512]{1,0:T(8,128)(2,1)S(1)} %get-tuple-element.12.ret_ref, ...), custom_call_target="tpu_custom_call" | custom-call | flops 402653184 | bytes 6291456 | tf_op jit(solution)/shard_map/pallas_call | solution.py:371
Async XLA Ops:
  2.2 1.6 %copy-start = (bf16[1,1024,1024]{2,1,0:T(8,128)(2,1)S(1)}, bf16[1,1024,1024]{2,1,0:T(8,128)(2,1)}, u32[]{:S(2)}) copy-start(bf16[1,1024,1024]{2,1,0:T(8,128)(2,1)} %wg_hbm.1) | copy-start | bytes 6291460
  3.8 1.6 %copy-start.1 = (bf16[1,1024,1024]{2,1,0:T(8,128)(2,1)S(1)}, bf16[1,1024,1024]{2,1,0:T(8,128)(2,1)}, u32[]{:S(2)}) copy-start(bf16[1,1024,1024]{2,1,0:T(8,128)(2,1)} %wu_hbm.1) | copy-start | bytes 6291460
  5.4 0.9 %copy-start.2 = (bf16[128,512]{1,0:T(8,128)(2,1)S(1)}, bf16[128,512]{1,0:T(8,128)(2,1)}, u32[]{:S(2)}) copy-start(bf16[128,512]{1,0:T(8,128)(2,1)} %tok_ref.1) | copy-start | bytes 393220
  6.3 0.9 %copy-start.3 = (bf16[128,512]{1,0:T(8,128)(2,1)S(1)}, bf16[128,512]{1,0:T(8,128)(2,1)}, u32[]{:S(2)}) copy-start(bf16[128,512]{1,0:T(8,128)(2,1)} %grad_ref.1) | copy-start | bytes 393220

commit v2 on v1

--- a/solution.py
+++ b/solution.py
@@ -9,7 +9,7 @@
 
 CAP = 16
 MESH = pl.DeviceIdType.MESH
-SUM_TYPE = jnp.float32
+SUM_TYPE = jnp.bfloat16
 CONTRACT_FIRST = (((0,), (0,)), ((), ()))
 CONTRACT_LAST = (((1,), (1,)), ((), ()))
 
@@ -40,10 +40,10 @@
 def exchange_kernel(
     ep,
     edp,
-    tok_ref,
-    grad_ref,
-    probs_ref,
-    ids_ref,
+    tok_hbm,
+    grad_hbm,
+    probs_hbm,
+    ids_hbm,
     wg_hbm,
     wu_hbm,
     wd_hbm,
@@ -57,10 +57,15 @@
     wg,
     wu,
     wd,
-    disp_t,
+    tok_ref,
+    grad_ref,
+    probs_ref,
+    ids_ref,
     pick_w,
     send_t,
     send_y,
+    mid_t,
+    mid_y,
     recv_t,
     recv_y,
     part,
@@ -74,6 +79,10 @@
     rs_t,
     ss_y,
     rs_y,
+    ss_tb,
+    rs_tb,
+    ss_yb,
+    rs_yb,
     ss_p,
     rs_p,
     ss_h,
@@ -85,15 +94,16 @@
     me_j = lax.axis_index("edp")
     per = edp // ep
     home = me_j // per
-    my_part = lax.rem(me_j, per)
     tok_rows, feat = tok_ref.shape
     slots = edp * CAP
     mine = pl.ds(pl.multiple_of(me_i * CAP, CAP), CAP)
     at_home = home == me_i
 
+    sources = (ids_hbm, probs_hbm, tok_hbm, grad_hbm, wg_hbm.at[0], wu_hbm.at[0], wd_hbm.at[0])
+    places = (ids_ref, probs_ref, tok_ref, grad_ref, wg, wu, wd)
     loads = [
-        pltpu.make_async_copy(src.at[0], dst, w_sem.at[n])
-        for n, (src, dst) in enumerate(((wg_hbm, wg), (wu_hbm, wu), (wd_hbm, wd)))
+        pltpu.make_async_copy(src, dst, w_sem.at[n])
+        for n, (src, dst) in enumerate(zip(sources, places))
     ]
     for load in loads:
         load.start()
@@ -120,72 +130,104 @@
 
     steps(edp, greet_experts)
     steps(edp, greet_owners)
+    for d in range(1, edp):
+        greet((me_i, lax.rem(me_j + d, edp)))
     for d in range(1, ep):
         greet((lax.rem(me_i + d, ep), me_j))
 
-    lane = lax.broadcasted_iota(jnp.int32, (tok_rows, slots), 1)
-    expert = lax.shift_right_logical(lane, 4)
-    place = lax.bitwise_and(lane, CAP - 1).astype(jnp.float32)
-    chosen = jnp.zeros((tok_rows, slots), jnp.float32)
-    weight = jnp.zeros((tok_rows, slots), jnp.float32)
-    for k in range(ids_ref.shape[1]):
-        hit = ids_ref[:, k : k + 1] == expert
+    slot = lax.broadcasted_iota(jnp.int32, (slots, tok_rows), 0)
+    expert = lax.shift_right_logical(slot, 4)
+    place = lax.bitwise_and(slot, CAP - 1).astype(jnp.float32)
+    chosen = jnp.zeros((slots, tok_rows), jnp.float32)
+    weight = jnp.zeros((slots, tok_rows), jnp.float32)
+    loads[0].wait()
+    loads[1].wait()
+    for k in range(ids_ref.shape[0]):
+        hit = ids_ref[k : k + 1, :] == expert
         chosen = jnp.where(hit, 1.0, chosen)
-        weight = jnp.where(hit, probs_ref[:, k : k + 1], weight)
+        weight = jnp.where(hit, probs_ref[k : k + 1, :], weight)
     row = lax.broadcasted_iota(jnp.int32, (tok_rows, tok_rows), 0)
     col = lax.broadcasted_iota(jnp.int32, (tok_rows, tok_rows), 1)
-    before = jnp.where(col < row, 1.0, 0.0).astype(jnp.bfloat16)
-    rank = dot_f32(before, chosen.astype(jnp.bfloat16))
+    before = jnp.where(row < col, 1.0, 0.0).astype(jnp.bfloat16)
+    rank = dot_f32(chosen.astype(jnp.bfloat16), before)
     disp = jnp.where(rank == place, chosen, 0.0)
     disp_out[...] = disp.astype(jnp.bfloat16)
-    disp_t[...] = disp.T.astype(jnp.bfloat16)
-    pick_w[...] = (disp * weight).T
-    send_t[...] = dot_f32(disp_t[...], tok_ref[...]).astype(jnp.bfloat16)
+    pick_w[...] = disp * weight
+    loads[2].wait()
+    send_t[...] = dot_f32(disp_out[...], tok_ref[...]).astype(jnp.bfloat16)
 
     @pl.when(at_home)
     def _():
-        pl.semaphore_wait(barrier, 2 * edp + ep - 1 - 2)
+        pl.semaphore_wait(barrier, 3 * edp - 1 + ep - 1 - 2)
 
     @pl.when(jnp.logical_not(at_home))
     def _():
-        pl.semaphore_wait(barrier, 2 * edp + ep - 1)
-
-    def dispatch(k, send, recv, send_sem, recv_sem, action):
-        e = lax.rem(me_j + 1 + k, edp)
-        here = jnp.logical_and(at_home, e == me_j)
-        src = send.at[pl.ds(pl.multiple_of(e * CAP, CAP), CAP), :]
-        dst = recv.at[my_part, mine, :]
-        arrive = recv_sem.at[my_part, me_i]
-
-        @pl.when(here)
-        def _():
-            if action == "start":
-                pltpu.make_async_copy(src, dst, arrive).start()
-
-        @pl.when(jnp.logical_not(here))
-        def _():
-            copy = remote(src, dst, send_sem.at[e], arrive, (home, e))
-            if action == "start":
-                copy.start()
-            else:
-                copy.wait_send()
-
-    def landed(k, recv, recv_sem):
-        i = k // per
-        p = lax.rem(k, per)
-        spot = recv.at[p, pl.ds(pl.multiple_of(i * CAP, CAP), CAP), :]
-        pltpu.make_async_copy(spot, spot, recv_sem.at[p, i]).wait()
-
-    steps(edp, lambda k: dispatch(k, send_t, recv_t, ss_t, rs_t, "start"))
-    send_y[...] = dot_f32(disp_t[...], grad_ref[...]).astype(jnp.bfloat16)
-    steps(edp, lambda k: dispatch(k, send_y, recv_y, ss_y, rs_y, "start"))
+        pl.semaphore_wait(barrier, 3 * edp - 1 + ep - 1)
+
+    def rows_of(first, count):
+        return pl.ds(pl.multiple_of(first * CAP, CAP), count * CAP)
+
+    def along_experts(d, send, mid, send_sem, recv_sem):
+        e = lax.rem(me_j + d, edp)
+        return remote(
+            send.at[rows_of(e, 1), :],
+            mid.at[rows_of(me_j, 1), :],
+            send_sem.at[d - 1],
+            recv_sem.at[d - 1],
+            (me_i, e),
+        )
+
+    def start_experts(send, mid, send_sem, recv_sem):
+        steps(edp - 1, lambda k: along_experts(k + 1, send, mid, send_sem, recv_sem).start())
+        mid[rows_of(me_j, 1), :] = send[rows_of(me_j, 1), :]
+
+    def along_blocks(d, mid, recv, send_sem, recv_sem):
+        to = lax.rem(me_i + d, ep)
+        return remote(
+            mid.at[rows_of(to * per, per), :],
+            recv.at[me_i],
+            send_sem.at[d - 1],
+            recv_sem.at[d - 1],
+            (to, me_j),
+        )
+
+    def came_from(i, mid, recv_sem):
+        for p in range(per):
+            j = i * per + p
+            spot = mid.at[rows_of(j, 1), :]
+
+            @pl.when(j != me_j)
+            def _():
+                n = lax.rem(me_j - j + edp, edp) - 1
+                pltpu.make_async_copy(spot, spot, recv_sem.at[n]).wait()
+
+    def forward(mid, recv, mid_sem, send_sem, recv_sem):
+        for d in range(1, ep):
+            came_from(lax.rem(me_i + d, ep), mid, mid_sem)
+            along_blocks(d, mid, recv, send_sem, recv_sem).start()
+        came_from(me_i, mid, mid_sem)
+        recv[me_i, :, :] = mid[rows_of(me_i * per, per), :]
+
+    def assemble(out, mid, recv, send_sem, recv_sem):
+        for d in range(1, ep):
+            along_blocks(d, mid, recv, send_sem, recv_sem).wait_recv()
+        for i in range(ep):
+            for p in range(per):
+                out[i * CAP : (i + 1) * CAP, p * feat : (p + 1) * feat] = recv[
+                    i, p * CAP : (p + 1) * CAP, :
+                ]
+
+    start_experts(send_t, mid_t, ss_t, rs_t)
+    loads[3].wait()
+    send_y[...] = dot_f32(disp_out[...], grad_ref[...]).astype(jnp.bfloat16)
+    start_experts(send_y, mid_y, ss_y, rs_y)
+    forward(mid_t, recv_t, rs_t, ss_tb, rs_tb)
 
     def share_sum(m, total):
+        send_p[m, :, :] = total.astype(SUM_TYPE)
+        for d in range(1, ep):
+            sum_copy(m, d).start()
         part[m, :, :] = total
-        if send_p is not part:
-            send_p[m, :, :] = total.astype(SUM_TYPE)
-        for d in range(1, ep):
-            sum_copy(m, d).start()
 
     def sum_copy(m, d):
         to = lax.rem(me_i + d, ep)
@@ -201,17 +243,14 @@
             total = total + recv_p[m, d - 1, :, :].astype(jnp.float32)
         return total
 
-    loads[0].wait()
-    steps(edp, lambda k: landed(k, recv_t, rs_t))
-    for p in range(per):
-        x_out[:, p * feat : (p + 1) * feat] = recv_t[p, :, :]
+    loads[4].wait()
+    assemble(x_out, mid_t, recv_t, ss_tb, rs_tb)
     share_sum(0, dot_f32(x_out[...], wg[...]))
-    loads[1].wait()
+    forward(mid_y, recv_y, rs_y, ss_yb, rs_yb)
+    loads[5].wait()
     share_sum(1, dot_f32(x_out[...], wu[...]))
-    loads[2].wait()
-    steps(edp, lambda k: landed(k, recv_y, rs_y))
-    for p in range(per):
-        y_out[:, p * feat : (p + 1) * feat] = recv_y[p, :, :]
+    loads[6].wait()
+    assemble(y_out, mid_y, recv_y, ss_yb, rs_yb)
     share_sum(2, dot_f32(y_out[...], wd[...], CONTRACT_LAST))
 
     own = pl.ds(pl.multiple_of(me_j * CAP, CAP), CAP)
@@ -281,8 +320,11 @@
     ug_out[...] = hid[1, :, :]
     hid_arrived(2)
     hw_out[...] = hid[2, :, :]
-    steps(edp, lambda k: dispatch(k, send_t, recv_t, ss_t, rs_t, "wait"))
-    steps(edp, lambda k: dispatch(k, send_y, recv_y, ss_y, rs_y, "wait"))
+    for args in ((send_t, mid_t, ss_t, rs_t), (send_y, mid_y, ss_y, rs_y)):
+        steps(edp - 1, lambda k: along_experts(k + 1, *args).wait_send())
+    for args in ((mid_t, recv_t, ss_tb, rs_tb), (mid_y, recv_y, ss_yb, rs_yb)):
+        for d in range(1, ep):
+            along_blocks(d, *args).wait_send()
     for m in range(3):
         for d in range(1, ep):
             sum_copy(m, d).wait_send()
@@ -298,24 +340,28 @@
     dg_ref[0, :, :] = dot_f32(x_ref[...], gg_ref[...], CONTRACT_FIRST).astype(jnp.bfloat16)
     du_ref[0, :, :] = dot_f32(x_ref[...], ug_ref[...], CONTRACT_FIRST).astype(jnp.bfloat16)
     dd_ref[0, :, :] = dot_f32(hw_ref[...], y_ref[...], CONTRACT_FIRST).astype(jnp.bfloat16)
-    tg_ref[...] = dot_f32(disp_ref[...], ret_ref[...]).astype(jnp.bfloat16)
+
+    @pl.when(pl.program_id(0) == 0)
+    def _():
+        tg_ref[...] = dot_f32(disp_ref[...], ret_ref[...], CONTRACT_FIRST).astype(jnp.bfloat16)
 
 
 def per_device(tokens, out_grad, probs, expert_ids, w_gate, w_up, w_down):
     ep, edp = lax.axis_size("ep"), lax.axis_size("edp")
     per = edp // ep
     tok_rows, feat = tokens.shape
+    picks = probs.shape[1]
     width, hidden = w_gate.shape[1:]
     slots = edp * CAP
     rows = ep * CAP
     bf16, f32 = jnp.bfloat16, jnp.float32
     vmem = pl.BlockSpec(memory_space=pltpu.VMEM)
-    anywhere = pl.BlockSpec(memory_space=pl.ANY)
+    hbm = pl.BlockSpec(memory_space=pltpu.HBM)
     dma = pltpu.SemaphoreType.DMA
     disp, ret, x_s, y_s, gg, ug, hw = pl.pallas_call(
         functools.partial(exchange_kernel, ep, edp),
         out_shape=[
-            jax.ShapeDtypeStruct((tok_rows, slots), bf16),
+            jax.ShapeDtypeStruct((slots, tok_rows), bf16),
             jax.ShapeDtypeStruct((slots, feat), bf16),
             jax.ShapeDtypeStruct((rows, width), bf16),
             jax.ShapeDtypeStruct((rows, width), bf16),
@@ -323,29 +369,38 @@
             jax.ShapeDtypeStruct((rows, hidden), bf16),
             jax.ShapeDtypeStruct((rows, hidden), bf16),
         ],
-        in_specs=[vmem] * 4 + [anywhere] * 3,
+        in_specs=[hbm] * 7,
         out_specs=[vmem] * 7,
         scratch_shapes=[
             pltpu.VMEM((width, hidden), bf16),
             pltpu.VMEM((width, hidden), bf16),
             pltpu.VMEM((hidden, width), bf16),
-            pltpu.VMEM((slots, tok_rows), bf16),
+            pltpu.VMEM((tok_rows, feat), bf16),
+            pltpu.VMEM((tok_rows, feat), bf16),
+            pltpu.VMEM((picks, tok_rows), f32),
+            pltpu.VMEM((picks, tok_rows), jnp.int32),
             pltpu.VMEM((slots, tok_rows), f32),
             pltpu.VMEM((slots, feat), bf16),
             pltpu.VMEM((slots, feat), bf16),
-            pltpu.VMEM((per, rows, feat), bf16),
-            pltpu.VMEM((per, rows, feat), bf16),
+            pltpu.VMEM((slots, feat), bf16),
+            pltpu.VMEM((slots, feat), bf16),
+            pltpu.VMEM((ep, per * CAP, feat), bf16),
+            pltpu.VMEM((ep, per * CAP, feat), bf16),
             pltpu.VMEM((3, rows, hidden), f32),
             pltpu.VMEM((3, rows, hidden), SUM_TYPE),
             pltpu.VMEM((3, ep - 1, CAP, hidden), SUM_TYPE),
             pltpu.VMEM((3, rows, hidden), bf16),
             pltpu.VMEM((per, rows, feat), bf16),
             pltpu.VMEM((slots, feat), bf16),
-            dma((3,)),
-            dma((edp,)),
-            dma((per, ep)),
-            dma((edp,)),
-            dma((per, ep)),
+            dma((7,)),
+            dma((edp - 1,)),
+            dma((edp - 1,)),
+            dma((edp - 1,)),
+            dma((edp - 1,)),
+            dma((ep - 1,)),
+            dma((ep - 1,)),
+            dma((ep - 1,)),
+            dma((ep - 1,)),
             dma((3, ep - 1)),
             dma((3, ep - 1)),
             dma((3, ep - 1)),
@@ -354,14 +409,14 @@
             dma((edp,)),
         ],
         compiler_params=pltpu.CompilerParams(
-            collective_id=0, has_side_effects=True, vmem_limit_bytes=48 * 1024 * 1024
+            collective_id=0, has_side_effects=True, vmem_limit_bytes=60 * 1024 * 1024
         ),
         cost_estimate=pl.CostEstimate(
             flops=10 * rows * width * hidden,
             bytes_accessed=6 * width * hidden,
             transcendentals=CAP * hidden,
         ),
-    )(tokens, out_grad, probs, expert_ids, w_gate, w_up, w_down)
+    )(tokens, out_grad, probs.T, expert_ids.T, w_gate, w_up, w_down)
 
     tiles = max(1, min(4, width // 128))
 
@@ -378,7 +433,7 @@
             jax.ShapeDtypeStruct((1, hidden, width), bf16),
         ],
         in_specs=[
-            pl.BlockSpec((tok_rows // tiles, slots), lambda n: (n, 0)),
+            whole((slots, tok_rows)),
             whole((slots, feat)),
             pl.BlockSpec((rows, width // tiles), lambda n: (0, n)),
             whole((rows, width)),
@@ -387,12 +442,12 @@
             pl.BlockSpec((rows, hidden // tiles), lambda n: (0, n)),
         ],
         out_specs=[
-            pl.BlockSpec((tok_rows // tiles, feat), lambda n: (n, 0)),
+            whole((tok_rows, feat)),
             pl.BlockSpec((1, width // tiles, hidden), lambda n: (0, n, 0)),
             pl.BlockSpec((1, width // tiles, hidden), lambda n: (0, n, 0)),
             pl.BlockSpec((1, hidden // tiles, width), lambda n: (0, n, 0)),
         ],
-        compiler_params=pltpu.CompilerParams(vmem_limit_bytes=32 * 1024 * 1024),
+        compiler_params=pltpu.CompilerParams(vmem_limit_bytes=60 * 1024 * 1024),
         cost_estimate=pl.CostEstimate(
             flops=6 * rows * width * hidden,
             bytes_accessed=6 * width * hidden,

time: 50.9 us -> 47.2 us (0.927)
  local copies, waits for them, and re-layouts: 6.56 us -> 0 us
  Pallas kernels: 43.4 us -> 46.4 us
    unnamed x10 -> x0, local copies, waits for them, and re-layouts: 6.56 us -> none
    pallas_call x1, Pallas kernels: 3.89 us -> 5.65 us  [per_device(): pl.pallas_call(grads_kernel, grid=(tiles,), out_shape=[jax.ShapeDtypeStru...]
    pallas_call x1, Pallas kernels: 39.5 us -> 40.7 us  [per_device(): pl.pallas_call(functools.partial(exchange_kernel, ep, edp), out_shape=[ja...]
where the time goes in v2:
time: 47.2 us; the launch traced here: 47 us
  Pallas kernels  46.4 us (98%)
  between operations  0.64 us (1%)
    pallas_call x1, Pallas kernels, per_device(): pl.pallas_call(functools.partial(exchange_kernel, ep, edp), out_shape=[ja...  40.7 us
    pallas_call x1, Pallas kernels, per_device(): pl.pallas_call(grads_kernel, grid=(tiles,), out_shape=[jax.ShapeDtypeStru...  5.65 us

profile of v2, /device:TPU:0, one launch (start us, length us, event | category | flops | bytes accessed | tf_op | source)
XLA Modules:
  0.0 47.0 jit_solution(4797150218419712409)
XLA Ops:
  0.6 40.7 %shard_map.102 = (bf16[128,128]{1,0:T(8,128)(2,1)}, bf16[128,512]{1,0:T(8,128)(2,1)}, bf16[64,1024]{1,0:T(8,128)(2,1)}, bf16[64,1024]{1,0:T(8,128)(2,1)}, bf16[6...) custom-call(bf16[128,512]{1,0:T(8,128)(2,1)} %tok_hbm.1, bf16[128,512]{1,0:T(8,128)(2,1)} %grad_hbm.1, ...), custom_call_target="tpu_custom_call" | custom-call | flops 671088640 | bytes 6291456 | tf_op jit(solution)/shard_map/pallas_call | solution.py:361
  41.4 5.7 %shard_map.103 = (bf16[128,512]{1,0:T(8,128)(2,1)}, bf16[1,1024,1024]{2,1,0:T(8,128)(2,1)}, bf16[1,1024,1024]{2,1,0:T(8,128)(2,1)}, bf16[1,1024,1024]{2,1,0:T(8,128)(2,1)}) custom-call(bf16[128,128]{1,0:T(8,128)(2,1)} %get-tuple-element.11.disp_ref, bf16[128,512]{1,0:T(8,128)(2,1)} %get-tuple-element.12.ret_ref, bf16[64,1024]{1,0:T(8,128)(2,1)} %get-tuple-element.13.x_ref, ...), custom_call_target="tpu_custom_call" | custom-call | flops 402653184 | bytes 6291456 | tf_op jit(solution)/shard_map/pallas_call | solution.py:426
